TPU v7x, 512 devices: a whole 4x8x8 slice. The times are simulated.
512 devices in a mesh: leaf: 32 (over z, x), front: 16 (over y, core).
Axes of the slice: x: 4, y: 8, z: 8, core: 2. Of those that a mesh axis runs over, the one named last changes fastest.
Arguments:
- rhs_child: float32 [32, 128, 2048], P('leaf', None, 'front'), may hold values from -8 to 8
- child_inverse: float32 [32, 2048, 2048], P('leaf', 'front'), as said below
- update_block: float32 [32, 1024, 2048], P('leaf', None, 'front'), may hold values from -0.125 to 0.125
- row_map: int32 [32, 1024], P('leaf'), may hold values from 0 to 8191, as said below
- rhs_root: float32 [128, 8192], P('front', 'leaf'), may hold values from -8 to 8
- root_inverse: float32 [8192, 8192], P('front', 'leaf'), as said below
Outputs:
- child_solution: float32 [32, 128, 2048], P('leaf', None, 'front')
- root_solution: float32 [128, 8192], P('front', 'leaf')
Inputs may be any that keep to these rules, and one draw needn't show every extreme that they name: `row_map`: each row holds 1024 distinct root rows, and every row names both 0 and 8191. `child_inverse`: each matrix is lower triangular with a positive diagonal. `root_inverse`: lower triangular with a positive diagonal.
All inputs are finite; a program needn't handle non-finite values.
Results may differ from a plain program's by a relative error of at most 0.000075.
Values sent between devices are 32-bit elements; how exact they have to be, the bound alone decides.
A program may use at most 64 MiB of HBM per device.

v0:
```python
import jax
import jax.numpy as jnp
from jax import lax
from jax.sharding import PartitionSpec as P

P_SIZE = 8192


def product(left, right):
    return jnp.dot(left, right, precision=lax.Precision.HIGHEST, preferred_element_type=jnp.float32)


def times_transposed(left, right):
    return lax.dot_general(
        left,
        right,
        (((1,), (1,)), ((), ())),
        precision=lax.Precision.HIGHEST,
        preferred_element_type=jnp.float32,
    )


def body(rhs_child, child_inverse, update_block, row_map, rhs_root, root_inverse):
    inverse_rows = child_inverse[0]
    update_rows = update_block[0]
    targets = row_map[0]
    frame_share = rhs_root.shape[0]
    columns = inverse_rows
    solved_child = times_transposed(
        lax.all_gather(rhs_child, "front", axis=2, tiled=True)[0], columns
    )
    update = lax.psum_scatter(
        times_transposed(solved_child, update_rows), "front", scatter_dimension=0, tiled=True
    )
    spread_rows = jnp.zeros((frame_share, P_SIZE), jnp.float32).at[:, targets].add(update)
    gathered_sum = lax.psum_scatter(spread_rows, "leaf", scatter_dimension=1, tiled=True)
    reduced = rhs_root - gathered_sum
    partial_value = times_transposed(
        lax.all_gather(reduced, "front", axis=0, tiled=True), root_inverse
    )
    solved_root = lax.psum(partial_value, "leaf")
    root_solution = lax.psum_scatter(
        product(solved_root, root_inverse), "front", scatter_dimension=0, tiled=True
    )
    columns = lax.all_gather(root_solution, "front", axis=0, tiled=True)
    complete = lax.all_gather(columns, "leaf", axis=1, tiled=True)
    picked = jnp.take(complete, targets, axis=1)
    residue = solved_child - product(picked, update_rows)
    child_solution = lax.psum_scatter(
        product(residue, inverse_rows), "front", scatter_dimension=1, tiled=True
    )
    return (child_solution[None], root_solution)


def solution(mesh):
    placed = (
        P("leaf", None, "front"),
        P("leaf", "front", None),
        P("leaf", None, "front"),
        P("leaf", None),
        P("front", "leaf"),
        P("front", "leaf"),
    )
    return jax.shard_map(
        body,
        mesh=mesh,
        in_specs=placed,
        out_specs=(P("leaf", None, "front"), P("front", "leaf")),
        check_vma=False,
    )
```

profile of v0, /device:TPU:1, one launch (start us, length us, event | category | flops | bytes accessed | tf_op | source)
XLA Modules:
  0.0 762.1 jit_solution(9227242060319772376)
XLA Ops:
  7.2 0.0 copy-start
  7.2 0.0 all-gather.3.cloned.1.call-start
  7.2 0.7 all-gather.3.cloned.1.call-update
  7.9 0.0 reduce-scatter.13.cloned.1.call-start
  8.0 48.1 %all-gather.3.cloned.1.call-done = f32[1,128,2048]{2,1,0:T(8,128)} async-done(((f32[1,128,128]{2,1,0:T(8,128)}), f32[1,128,2048]{2,1,0:T(8,128)}) %all-gather.3.cloned.1.call-update) | async-done | bytes 1048592 | tf_op jit(solution)/shard_map/all_gather | solution.py:30
  56.1 0.0 copy-done
  56.1 2.2 fusion.4
  58.3 2.4 fusion.9
  60.7 0.0 reduce-scatter.13.cloned.1.call-update
  60.7 0.0 reduce-scatter.7.cloned.1.call-start
  60.8 0.7 compare_select_fusion
  61.5 55.6 %reduce-scatter.13.cloned.1.call-done = f32[8,1024]{1,0:T(8,128)} async-done(((f32[128,1024]{1,0:T(8,128)}), f32[8,1024]{1,0:T(8,128)}) %reduce-scatter.13.cloned.1.call-update) | async-done | bytes 32784
  117.0 0.9 copy.21
  118.0 0.0 copy-start.4
  118.0 0.0 copy-start.1
  118.0 8.2 %scatter_custom_fusion = f32[8,8192]{0,1:T(8,128)} fusion(s32[1024]{0:T(1024)S(1)} %bitcast.29, f32[]{:T(128)} %constant.18.clone.1, f32[8,1024]{0,1:T(8,128)S(1)} %copy.21), kind=kCustom, calls=%fused_computation.2 | custom fusion | flops 8192 | bytes 786436 | tf_op jit(solution)/shard_map/scatter-add | solution.py:35
  126.2 0.0 copy-start.3
  126.2 3.5 copy.17
  129.7 0.0 reduce-scatter.7.cloned.1.call-update
  129.7 0.0 all-reduce.2.cloned.1.call-start
  129.8 214.5 %reduce-scatter.7.cloned.1.call-done = f32[8,256]{1,0:T(8,128)} async-done(((f32[8,8192]{1,0:T(8,128)}), f32[8,256]{1,0:T(8,128)}) %reduce-scatter.7.cloned.1.call-update) | async-done | bytes 8208 | tf_op jit(solution)/shard_map/reduce_scatter | solution.py:36
  344.3 0.0 copy-done.4
  344.3 0.7 sub.6
  345.0 23.0 %all_gather.13 = f32[128,256]{1,0:T(8,128)S(1)} all-gather(f32[8,256]{1,0:T(8,128)S(1)} %sub.6), channel_id=1, replica_groups=mesh['leaf'=32,'front'=16] {'front'}, dimensions={0}, use_global_device_ids=true | all-gather | bytes 139264 | tf_op jit(solution)/shard_map/all_gather | solution.py:39
  367.9 0.0 copy-done.1
  367.9 1.3 fusion.15
  369.3 0.0 all-reduce.2.cloned.1.call-update
  369.3 0.0 reduce-scatter.9.cloned.1.call-start
  369.3 146.2 %all-reduce.2.cloned.1.call-done = f32[128,512]{1,0:T(8,128)} async-done(((f32[128,512]{1,0:T(8,128)}), f32[128,512]{1,0:T(8,128)}) %all-reduce.2.cloned.1.call-update) | async-done | bytes 262160 | tf_op jit(solution)/shard_map/psum | solution.py:41
  515.6 2.0 fusion.16
  517.6 0.0 reduce-scatter.9.cloned.1.call-update
  517.6 0.0 all-gather.5.cloned.1.call-start
  517.6 58.7 %reduce-scatter.9.cloned.1.call-done = f32[8,256]{1,0:T(8,128)} async-done(((f32[128,256]{1,0:T(8,128)}), f32[8,256]{1,0:T(8,128)}) %reduce-scatter.9.cloned.1.call-update) | async-done | bytes 8208 | tf_op jit(solution)/shard_map/reduce_scatter | solution.py:42
  576.3 18.3 %all_gather.14 = f32[128,256]{1,0:T(8,128)} all-gather(f32[8,256]{1,0:T(8,128)} %reduce-scatter.9.cloned.1.call-done), channel_id=1, replica_groups=mesh['leaf'=32,'front'=16] {'front'}, dimensions={0}, use_global_device_ids=true | all-gather | bytes 139264 | tf_op jit(solution)/shard_map/all_gather | solution.py:45
  594.7 0.0 all-gather.5.cloned.1.call-update
  594.7 0.0 reduce-scatter.11.cloned.1.call-start
  594.7 0.0 copy-done.3
  594.8 85.4 %all-gather.5.cloned.1.call-done = f32[128,8192]{1,0:T(8,128)} async-done(((f32[128,256]{1,0:T(8,128)}), f32[128,8192]{1,0:T(8,128)}) %all-gather.5.cloned.1.call-update) | async-done | bytes 4194320 | tf_op jit(solution)/shard_map/all_gather | solution.py:46
  680.1 5.6 copy.18
  685.7 0.0 copy-start.2
  685.7 5.0 gather_fusion
  690.8 0.0 copy-done.2
  690.8 1.2 convolution_subtract_fusion
  692.0 2.0 fusion.2
  694.0 0.0 reduce-scatter.11.cloned.1.call-update
  694.0 61.2 %reduce-scatter.11.cloned.1.call-done = f32[128,128]{1,0:T(8,128)} async-done(((f32[128,2048]{1,0:T(8,128)}), f32[128,128]{1,0:T(8,128)}) %reduce-scatter.11.cloned.1.call-update) | async-done | bytes 65552 | tf_op jit(solution)/shard_map/reduce_scatter | solution.py:49
  (2 shorter events, 0.0 us)
Async XLA Ops:
  7.2 48.9 %copy-start = (f32[1,128,2048]{2,1,0:T(8,128)S(1)}, f32[1,128,2048]{2,1,0:T(8,128)}, u32[]{:S(2)}) copy-start(f32[1,128,2048]{2,1,0:T(8,128)} %param.7) | copy-start | bytes 3145732
  7.2 48.9 %all-gather.3.cloned.1.call-start = ((), (), s32[]{:S(2)}) async-start(), calls=%async_computation.4 | async-start | bytes 1114112 | tf_op jit(solution)/shard_map/all_gather | solution.py:30
  7.9 109.1 %reduce-scatter.13.cloned.1.call-start = ((), (), s32[]{:S(2)}) async-start(), calls=%async_computation.10 | async-start | bytes 557056
  60.7 283.5 %reduce-scatter.7.cloned.1.call-start = ((), (), s32[]{:S(2)}) async-start(), calls=%async_computation.5 | async-start | bytes 270336 | tf_op jit(solution)/shard_map/reduce_scatter | solution.py:36
  118.0 226.3 %copy-start.4 = (f32[8,256]{1,0:T(8,128)S(1)}, f32[8,256]{1,0:T(8,128)}, u32[]{:S(2)}) copy-start(f32[8,256]{1,0:T(8,128)} %param.10) | copy-start | bytes 24580
  118.0 249.9 %copy-start.1 = (f32[512,256]{1,0:T(8,128)S(1)}, f32[512,256]{1,0:T(8,128)}, u32[]{:S(2)}) copy-start(f32[512,256]{1,0:T(8,128)} %param.11) | copy-start | bytes 1572868
  126.2 468.5 %copy-start.3 = (s32[1,1024]{1,0:T(1,128)S(1)}, s32[1,1024]{1,0:T(1,128)}, u32[]{:S(2)}) copy-start(s32[1,1024]{1,0:T(1,128)} %param.9) | copy-start | bytes 12292
  129.7 385.9 %all-reduce.2.cloned.1.call-start = ((), (), s32[]{:S(2)}) async-start(), calls=%async_computation.6 | async-start | bytes 524288 | tf_op jit(solution)/shard_map/psum | solution.py:41
  369.3 207.0 %reduce-scatter.9.cloned.1.call-start = ((), (), s32[]{:S(2)}) async-start(), calls=%async_computation.7 | async-start | bytes 139264 | tf_op jit(solution)/shard_map/reduce_scatter | solution.py:42
  517.6 162.5 %all-gather.5.cloned.1.call-start = ((), (), s32[]{:S(2)}) async-start(), calls=%async_computation.8 | async-start | bytes 4325376 | tf_op jit(solution)/shard_map/all_gather | solution.py:46
  594.7 160.5 %reduce-scatter.11.cloned.1.call-start = ((), (), s32[]{:S(2)}) async-start(), calls=%async_computation.9 | async-start | bytes 1114112 | tf_op jit(solution)/shard_map/reduce_scatter | solution.py:49
  685.7 5.1 copy-start.2
Sparse Core Ops, SparseCore 0:
  10.1 45.9 all-gather.2
  60.9 56.1 reduce-scatter.12
  129.8 214.3 reduce-scatter.6
  369.4 146.1 all-reduce.1
  518.8 57.5 reduce-scatter.8
  594.8 85.2 all-gather.4
  694.1 61.0 reduce-scatter.10
where the time goes:
time: 763 us; the launch traced here: 762 us
  waiting for transfers between devices  670 us (88%)
  blocking collectives  41.3 us (5%)
  local copies, waits for them, and re-layouts  15.1 us (2%)
  between operations  14.2 us (2%)
  matrix products  11.1 us (1%)
  other arithmetic  9.62 us (1%)
    reduce_scatter x1, waiting for transfers between devices, body(): lax.psum_scatter(spread_rows, 'leaf', scatter_dimension=1, tiled=True)  214 us
    psum x1, waiting for transfers between devices, body(): solved_root = lax.psum(partial_value, 'leaf')  146 us
    all_gather x1, waiting for transfers between devices, body(): complete = lax.all_gather(columns, 'leaf', axis=1, tiled=True)  85.4 us
    reduce_scatter x1, waiting for transfers between devices, body(): lax.psum_scatter(product(residue, inverse_rows), 'front', scatter_dimensi...  61.2 us
    reduce_scatter x1, waiting for transfers between devices, body(): lax.psum_scatter(product(solved_root, root_inverse), 'front', scatter_dim...  58.7 us
    unnamed x8, waiting for transfers between devices  56.3 us
    all_gather x1, waiting for transfers between devices, body(): lax.all_gather(rhs_child, 'front', axis=2, tiled=True)[0]  48.1 us
    all_gather x1, blocking collectives, body(): lax.all_gather(reduced, 'front', axis=0, tiled=True)  23 us
  transfers between devices with their start and end apart: 7, of which 7 were waited for; matrix products, arithmetic and copies ran while one was open for 0% of the time, Pallas kernels for 0%

commit v1 on v0

v1 whole, which is shorter than its diff:
```python
import functools

import jax
import jax.numpy as jnp
from jax import lax
from jax.experimental import pallas as pl
from jax.experimental.pallas import tpu as pltpu
from jax.sharding import PartitionSpec as P

MESH = pl.DeviceIdType.MESH
F32 = jnp.float32
BF16 = jnp.bfloat16
NN = (((1,), (0,)), ((), ()))
NT = (((1,), (1,)), ((), ()))


def split2(x):
    hi = x.astype(BF16)
    return hi, (x - hi.astype(F32)).astype(BF16)


def split3(x):
    hi = x.astype(BF16)
    rest = x - hi.astype(F32)
    mid = rest.astype(BF16)
    return hi, mid, (rest - mid.astype(F32)).astype(BF16)


def mul(a, b, dims):
    return lax.dot_general(a, b, dims, preferred_element_type=F32)


def mul3(a, bh, bl, dims):
    ah, al = split2(a)
    return mul(ah, bh, dims) + (mul(ah, bl, dims) + mul(al, bh, dims))


def kernel(
    nl, nf,
    rhs_c, inv, upd, rmap, rhs_r, rinv,
    child_out, root_out,
    gath, inv_h, inv_l, upd_h, upd_l, rinv_h, rinv_l, onehot, solved,
    b_send, b_pair, b_own, b_recv,
    c_send, c_recv, d_buf, e_send, e_recv, f_buf, g_send, g_recv, h_buf, i_buf,
    j_send, j_pair, j_own, j_recv,
    s_sem, r_sem, fs_sem, fr_sem, is_sem, ir_sem,
):
    ny, nh = nf // 2, nl // nf
    l = lax.axis_index("leaf")
    f = lax.axis_index("front")
    y, c = f // 2, f % 2
    sib = y * 2 + (1 - c)
    rows, width = rhs_r.shape
    frames = rows * nf
    ks, ku = rhs_c.shape[1], upd.shape[0]

    barrier = pltpu.get_barrier_semaphore()
    for d in range(1, nf):
        pl.semaphore_signal(barrier, inc=1, device_id={"front": (f + d) % nf}, device_id_type=MESH)
    for d in range(1, nl):
        pl.semaphore_signal(barrier, inc=1, device_id={"leaf": (l + d) % nl}, device_id_type=MESH)
    pl.semaphore_wait(barrier, nf + nl - 2)

    pending = []

    def send(src, dst, ss, rs, where):
        copy = pltpu.make_async_remote_copy(
            src_ref=src, dst_ref=dst, send_sem=ss, recv_sem=rs, device_id=where, device_id_type=MESH
        )
        copy.start()
        return copy

    def spread(count, axis, me, src, dst, k):
        for d in range(1, count):
            at = (me + d) % count
            send(src(at), dst(d), s_sem.at[k], r_sem.at[k], {axis: at})

    def wait_recv(ref, sem):
        pltpu.make_async_remote_copy(
            src_ref=ref, dst_ref=ref, send_sem=sem, recv_sem=sem, device_id={"front": sib}, device_id_type=MESH
        ).wait_recv()

    def wait_send(ref, sem):
        pltpu.make_async_remote_copy(
            src_ref=ref, dst_ref=ref, send_sem=sem, recv_sem=sem, device_id={"front": sib}, device_id_type=MESH
        ).wait_send()

    def finish():
        for ref, sem in pending:
            wait_send(ref, sem)

    send(rhs_c, gath.at[f], fs_sem.at[0], fr_sem.at[0], {"front": sib})
    pending.append((rhs_c, fs_sem.at[0]))
    for d in range(1, ny):
        at = ((y + d) % ny) * 2 + c
        send(rhs_c, gath.at[f], is_sem.at[d - 1], ir_sem.at[d - 1], {"front": at})
        pending.append((rhs_c, is_sem.at[d - 1]))
    gath[f] = rhs_c[...]
    for k in range(2):
        part = jnp.concatenate([inv[:, (2 * j + k) * ks : (2 * j + k + 1) * ks] for j in range(ny)], axis=1)
        inv_h[k], inv_l[k] = split2(part)
    upd_h[...], upd_l[...] = split2(upd[...])
    rinv_h[...], rinv_l[...] = split2(rinv[...])
    target = rmap[...]
    low = target % width
    high = target // width
    onehot[...] = jnp.where(lax.broadcasted_iota(jnp.int32, (width, ku), 0) == low, 1.0, 0.0).astype(BF16)
    pick_mask = lambda: lax.broadcasted_iota(jnp.int32, (nl, rows, ku), 0) == high[None]

    for d in range(1, ny):
        came = ((y + ny - d) % ny) * 2 + c
        wait_recv(gath.at[came], ir_sem.at[d - 1])
        send(gath.at[came], gath.at[came], fs_sem.at[d], fr_sem.at[d], {"front": sib})
        pending.append((gath.at[came], fs_sem.at[d]))
    for d in range(ny):
        wait_recv(gath.at[0], fr_sem.at[d])
    total = None
    for k in range(2):
        part = mul3(jnp.concatenate([gath[2 * j + k] for j in range(ny)], axis=1), inv_h[k], inv_l[k], NT)
        total = part if total is None else total + part
    by_core = total.reshape(ny, 2, rows, ks)
    for k in range(2):
        solved[k] = by_core[:, k].reshape(ny * rows, ks)

    b_send[...] = mul3(solved[1 - c], upd_h[...], upd_l[...], NT).reshape(ny, rows, ku)
    send(b_send, b_pair, s_sem.at[0], r_sem.at[0], {"front": sib})
    pending.append((b_send, s_sem.at[0]))
    mine = mul3(solved[c], upd_h[...], upd_l[...], NT).reshape(ny, rows, ku)
    wait_recv(b_pair, r_sem.at[0])
    b_own[...] = mine + b_pair[...]
    for d in range(1, ny):
        at = (y + d) % ny
        send(b_own.at[at], b_recv.at[d - 1], s_sem.at[1], r_sem.at[1], {"front": at * 2 + c})
    pending.append((b_recv, s_sem.at[1]))
    wait_recv(b_recv, r_sem.at[1])
    update = b_own[y] + jnp.sum(b_recv[...], axis=0)

    mask = pick_mask()
    parts = [
        jnp.where(mask, jnp.broadcast_to(p.astype(F32)[None], (nl, rows, ku)), 0.0).reshape(nl * rows, ku).astype(BF16)
        for p in split3(update)
    ]
    c_send[...] = (
        mul(parts[0], onehot[...], NT) + (mul(parts[1], onehot[...], NT) + mul(parts[2], onehot[...], NT))
    ).reshape(nl, rows, width)
    spread(nl, "leaf", l, lambda at: c_send.at[at], lambda d: c_recv.at[d - 1], 2)
    pending.append((c_recv, s_sem.at[2]))
    wait_recv(c_recv, r_sem.at[2])
    reduced = rhs_r[...] - (c_send[l] + jnp.sum(c_recv[...], axis=0))

    d_buf[f] = reduced
    spread(nf, "front", f, lambda at: d_buf.at[f], lambda d: d_buf.at[f], 3)
    pending.append((d_buf.at[pl.ds(0, nf - 1)], s_sem.at[3]))
    wait_recv(d_buf.at[pl.ds(0, nf - 1)], r_sem.at[3])

    part = mul3(d_buf[...].reshape(frames, width), rinv_h[...], rinv_l[...], NT)
    for h in range(nh):
        e_send[h] = part[:, h * width : (h + 1) * width].reshape(nf, rows, width)
    spread(nl, "leaf", l, lambda at: e_send.at[at % nh, at // nh], lambda d: e_recv.at[d - 1], 4)
    pending.append((e_recv, s_sem.at[4]))
    wait_recv(e_recv, r_sem.at[4])
    place = (l % nh) * nf + l // nh
    f_buf[place] = e_send[l % nh, l // nh] + jnp.sum(e_recv[...], axis=0)

    spread(nl, "leaf", l, lambda at: f_buf.at[place], lambda d: f_buf.at[place], 5)
    pending.append((f_buf.at[pl.ds(0, nl - 1)], s_sem.at[5]))
    wait_recv(f_buf.at[pl.ds(0, nl - 1)], r_sem.at[5])
    root = jnp.concatenate([f_buf[h * nf : (h + 1) * nf].reshape(frames, width) for h in range(nh)], axis=1)

    g_send[...] = mul3(root, rinv_h[...], rinv_l[...], NN).reshape(nf, rows, width)
    spread(nf, "front", f, lambda at: g_send.at[at], lambda d: g_recv.at[d - 1], 6)
    pending.append((g_recv, s_sem.at[6]))
    wait_recv(g_recv, r_sem.at[6])
    answer = g_send[f] + jnp.sum(g_recv[...], axis=0)
    h_buf[l] = answer

    spread(nl, "leaf", l, lambda at: h_buf.at[l], lambda d: h_buf.at[l], 7)
    pending.append((h_buf.at[pl.ds(0, nl - 1)], s_sem.at[7]))
    root_out[...] = answer
    wait_recv(h_buf.at[pl.ds(0, nl - 1)], r_sem.at[7])
    hh, hm, hl = split3(h_buf[...].reshape(nl * rows, width))
    chosen = mul(hh, onehot[...], NN) + (mul(hm, onehot[...], NN) + mul(hl, onehot[...], NN))
    picked = jnp.sum(jnp.where(pick_mask(), chosen.reshape(nl, rows, ku), 0.0), axis=0)

    i_buf[f] = picked
    send(i_buf.at[f], i_buf.at[f], fs_sem.at[ny], fr_sem.at[ny], {"front": sib})
    pending.append((i_buf.at[f], fs_sem.at[ny]))
    for d in range(1, ny):
        at = ((y + d) % ny) * 2 + c
        send(i_buf.at[f], i_buf.at[f], is_sem.at[ny - 1 + d - 1], ir_sem.at[ny - 1 + d - 1], {"front": at})
        pending.append((i_buf.at[f], is_sem.at[ny - 1 + d - 1]))
    for d in range(1, ny):
        came = ((y + ny - d) % ny) * 2 + c
        wait_recv(i_buf.at[came], ir_sem.at[ny - 1 + d - 1])
        send(i_buf.at[came], i_buf.at[came], fs_sem.at[ny + d], fr_sem.at[ny + d], {"front": sib})
        pending.append((i_buf.at[came], fs_sem.at[ny + d]))
    for d in range(ny):
        wait_recv(i_buf.at[0], fr_sem.at[ny + d])
    taken = mul3(i_buf[...].reshape(frames, ku), upd_h[...], upd_l[...], NN)
    first = [solved[k].reshape(ny, rows, ks) for k in range(2)]
    before = jnp.stack(first, axis=1).reshape(frames, ks)
    residue = before - taken

    for k in range(2):
        @pl.when(c == 1 - k)
        def _():
            other = mul3(residue, inv_h[k], inv_l[k], NN)
            for j in range(ny):
                j_send[j] = other[:, j * ks : (j + 1) * ks]
    send(j_send, j_pair, s_sem.at[8], r_sem.at[8], {"front": sib})
    pending.append((j_send, s_sem.at[8]))
    mine = mul3(residue, inv_h[c], inv_l[c], NN)
    wait_recv(j_pair, r_sem.at[8])
    for j in range(ny):
        j_own[j] = mine[:, j * ks : (j + 1) * ks] + j_pair[j]
    for d in range(1, ny):
        at = (y + d) % ny
        send(j_own.at[at], j_recv.at[d - 1], s_sem.at[9], r_sem.at[9], {"front": at * 2 + c})
    pending.append((j_recv, s_sem.at[9]))
    wait_recv(j_recv, r_sem.at[9])
    child_out[...] = j_own[y] + jnp.sum(j_recv[...], axis=0)
    finish()


def body(nl, nf, rhs_child, child_inverse, update_block, row_map, rhs_root, root_inverse):
    ny = nf // 2
    frames, ks = rhs_child.shape[1:]
    ku = update_block.shape[1]
    rows, width = rhs_root.shape
    deep = root_inverse.shape[0]
    vm = pltpu.VMEM
    scratch = [
        vm((nf, frames, ks), F32),
        vm((2, ks, ny * ks), BF16), vm((2, ks, ny * ks), BF16),
        vm((ku, ks), BF16), vm((ku, ks), BF16),
        vm((deep, width), BF16), vm((deep, width), BF16),
        vm((width, ku), BF16),
        vm((2, ny * rows, ks), F32),
        vm((ny, rows, ku), F32), vm((ny, rows, ku), F32), vm((ny, rows, ku), F32), vm((ny - 1, rows, ku), F32),
        vm((nl, rows, width), F32), vm((nl - 1, rows, width), F32),
        vm((nf, rows, width), F32),
        vm((nl // nf, nf, rows, width), F32), vm((nl - 1, rows, width), F32),
        vm((nl, rows, width), F32),
        vm((nf, rows, width), F32), vm((nf - 1, rows, width), F32),
        vm((nl, rows, width), F32),
        vm((nf, rows, ku), F32),
        vm((ny, frames, ks), F32), vm((ny, frames, ks), F32), vm((ny, frames, ks), F32), vm((ny - 1, frames, ks), F32),
        pltpu.SemaphoreType.DMA((10,)), pltpu.SemaphoreType.DMA((10,)),
        pltpu.SemaphoreType.DMA((2 * ny,)), pltpu.SemaphoreType.DMA((2 * ny,)),
        pltpu.SemaphoreType.DMA((2 * ny - 2,)), pltpu.SemaphoreType.DMA((2 * ny - 2,)),
    ]
    child, root = pl.pallas_call(
        functools.partial(kernel, nl, nf),
        out_shape=(
            jax.ShapeDtypeStruct((frames, ks), F32),
            jax.ShapeDtypeStruct((rows, width), F32),
        ),
        in_specs=[pl.BlockSpec(memory_space=pltpu.VMEM)] * 6,
        out_specs=(pl.BlockSpec(memory_space=pltpu.VMEM),) * 2,
        scratch_shapes=scratch,
        compiler_params=pltpu.CompilerParams(
            collective_id=0, has_side_effects=True, vmem_limit_bytes=48 * 1024 * 1024
        ),
    )(rhs_child[0], child_inverse[0], update_block[0], row_map, rhs_root, root_inverse)
    return child[None], root


def solution(mesh):
    placed = (
        P("leaf", None, "front"),
        P("leaf", "front", None),
        P("leaf", None, "front"),
        P("leaf", None),
        P("front", "leaf"),
        P("front", "leaf"),
    )
    return jax.shard_map(
        functools.partial(body, mesh.shape["leaf"], mesh.shape["front"]),
        mesh=mesh,
        in_specs=placed,
        out_specs=(P("leaf", None, "front"), P("front", "leaf")),
        check_vma=False,
    )
```

time: 763 us -> 128 us (0.17)
  waiting for transfers between devices: 670 us -> 0 us
  Pallas kernels: 0 us -> 118 us
  blocking collectives: 41.3 us -> 0 us
  between operations: 14.2 us -> 0.65 us
  matrix products: 11.1 us -> 0 us
  other arithmetic: 9.62 us -> 0 us
  local copies, waits for them, and re-layouts: 15.1 us -> 6.75 us
    reduce_scatter x3 -> x0, waiting for transfers between devices: 334 us -> none  [the longest x1 214 us: body(): lax.psum_scatter(spread_rows, 'leaf', scatter_dimension=1, tiled=True)]
    psum x1 -> x0, waiting for transfers between devices: 146 us -> none  [body(): solved_root = lax.psum(partial_value, 'leaf')]
    all_gather x2 -> x0, waiting for transfers between devices: 133 us -> none  [the longest x1 85.4 us: body(): complete = lax.all_gather(columns, 'leaf', axis=1, tiled=True)]
    pallas_call x0 -> x1, Pallas kernels: none -> 118 us  [body(): pl.pallas_call(functools.partial(kernel, nl, nf), out_shape=(jax.ShapeDty...]
    unnamed x8 -> x0, waiting for transfers between devices: 56.3 us -> none
    all_gather x2 -> x0, blocking collectives: 41.3 us -> none  [the longest x1 23 us: body(): lax.all_gather(reduced, 'front', axis=0, tiled=True)]
    dot_general x5 -> x0, matrix products: 8.71 us -> none  [the longest x3 5.15 us: product(): jnp.dot(left, right, precision=lax.Precision.HIGHEST, preferred_element_t...]
    scatter-add x1 -> x0, other arithmetic: 8.21 us -> none  [body(): jnp.zeros((frame_share, P_SIZE), jnp.float32).at[:, targets].add(update)]
  transfers between devices with their start and end apart: 7 -> 0, of which waited for: 7 -> 0; matrix products, arithmetic and copies ran while one was open for 0% -> 0% of each run, Pallas kernels for 0% -> 0%
where the time goes in v1:
time: 128 us; the launch traced here: 125 us
  Pallas kernels  118 us (92%)
  local copies, waits for them, and re-layouts  6.75 us (5%)
    pallas_call x1, Pallas kernels, body(): pl.pallas_call(functools.partial(kernel, nl, nf), out_shape=(jax.ShapeDty...  118 us
    unnamed x14, local copies, waits for them, and re-layouts  6.75 us

profile of v1, /device:TPU:1, one launch (start us, length us, event | category | flops | bytes accessed | tf_op | source)
XLA Modules:
  0.0 125.4 jit_solution(13773987832556883163)
XLA Ops:
  0.6 0.0 copy-start.5
  0.6 0.7 copy-done.5
  1.3 0.0 copy-start
  1.3 1.2 copy-done
  2.5 0.0 copy-start.1
  2.5 1.0 copy-done.1
  3.6 0.0 copy-start.2
  3.6 1.0 copy-done.2
  4.6 0.0 copy-start.3
  4.6 0.8 copy-done.3
  5.5 0.0 copy-start.4
  5.5 0.7 copy-done.4
  6.2 117.9 %shard_map.77 = (f32[128,128]{1,0:T(8,128)S(1)}, f32[8,256]{1,0:T(8,128)S(1)}) custom-call(f32[128,128]{1,0:T(8,128)S(1)} %bitcast.6, f32[128,2048]{1,0:T(8,128)S(1)} %bitcast.4, f32[1024,128]{1,0:T(8,128)S(1)} %bitcast.5, s32[1,1024]{1,0:T(1,128)S(1)} %copy-done.5, f32[8,256]{1,0:T(8,128)S(1)} %copy-done.4, f32[512,256]{1,0:T(8,128)S(1)} %copy-done.2), custom_call_target="tpu_custom_call" | custom-call | tf_op jit(solution)/shard_map/pallas_call | solution.py:252
  124.1 0.6 copy.10
  124.8 0.6 copy.11
Async XLA Ops:
  0.6 0.7 copy-start.5
  1.3 1.2 copy-start
  2.5 1.0 copy-start.1
  3.6 1.0 copy-start.2
  4.6 0.8 copy-start.3
  5.5 0.7 copy-start.4

commit v2 on v0

v2 whole, which is shorter than its diff:
```python
import functools

import jax
import jax.numpy as jnp
from jax import lax
from jax.experimental import pallas as pl
from jax.experimental.pallas import tpu as pltpu
from jax.sharding import PartitionSpec as P

NX = 4
MESH = pl.DeviceIdType.MESH
F32 = jnp.float32
BF16 = jnp.bfloat16
NN = (((1,), (0,)), ((), ()))
NT = (((1,), (1,)), ((), ()))


def split2(x):
    hi = x.astype(BF16)
    return hi, (x - hi.astype(F32)).astype(BF16)


def split3(x):
    hi = x.astype(BF16)
    rest = x - hi.astype(F32)
    mid = rest.astype(BF16)
    return hi, mid, (rest - mid.astype(F32)).astype(BF16)


def mul(a, b, dims):
    return lax.dot_general(a, b, dims, preferred_element_type=F32)


def mul3(a, bh, bl, dims):
    ah, al = split2(a)
    return mul(ah, bh, dims) + (mul(ah, bl, dims) + mul(al, bh, dims))


def ring_hops(d, n):
    return min(d, n - d)


def kernel(
    nl, nf,
    rhs_c, inv, upd, rmap, rhs_r, rinv,
    child_out, root_out,
    rhs_v, inv_v, upd_v, rinv_v, map_v, rr_v,
    gath, acc, inv_h, inv_l, upd_h, upd_l, rinv_h, rinv_l, onehot,
    b_send, b_pair, b_own, b_recv, c_send, c_recv, d_buf, e_send, e_recv, f_buf,
    g_send, g_recv, h_buf, i_buf, j_send, j_pair, j_own, j_recv,
    in_sem, a_ss, a_rs, af_ss, af_rs, i_ss, i_rs, if_ss, if_rs, s_sem, r_sem, g_ss, j_ss, j_rs,
):
    ny = nf // 2
    nz = nl // NX
    l = lax.axis_index("leaf")
    f = lax.axis_index("front")
    y, c = f // 2, f % 2
    z, x = l // NX, l % NX
    sib = y * 2 + (1 - c)
    rows, width = rr_v.shape
    ks, ku = acc.shape[2], upd_v.shape[0]
    half = ny * rows
    piece = e_recv.shape[-1]
    nq = e_send.shape[1]

    far_y = sorted(range(1, ny), key=lambda d: -ring_hops(d, ny))
    near_y = sorted(range(1, ny), key=lambda d: ring_hops(d, ny))
    far_l = sorted(
        [(dz, dx) for dz in range(nz) for dx in range(NX) if dz or dx],
        key=lambda d: -(ring_hops(d[0], nz) + ring_hops(d[1], NX)),
    )

    loads = [
        pltpu.make_async_copy(src, dst, in_sem.at[k])
        for k, (src, dst) in enumerate(
            [(rhs_c, rhs_v), (inv, inv_v), (upd, upd_v), (rmap, map_v), (rinv, rinv_v), (rhs_r, rr_v)]
        )
    ]
    for load in loads:
        load.start()
    barrier = pltpu.get_barrier_semaphore()
    for d in range(1, nf):
        pl.semaphore_signal(barrier, inc=1, device_id={"front": (f + d) % nf}, device_id_type=MESH)
    for d in range(1, nl):
        pl.semaphore_signal(barrier, inc=1, device_id={"leaf": (l + d) % nl}, device_id_type=MESH)
    loads[0].wait()
    pl.semaphore_wait(barrier, nf + nl - 2)

    pending = []

    def send(src, dst, ss, rs, where, when=None):
        pltpu.make_async_remote_copy(
            src_ref=src, dst_ref=dst, send_sem=ss, recv_sem=rs, device_id=where, device_id_type=MESH
        ).start()

    def both(ref, sem):
        return pltpu.make_async_remote_copy(
            src_ref=ref, dst_ref=ref, send_sem=sem, recv_sem=sem, device_id={"front": sib}, device_id_type=MESH
        )

    def wait_recv(ref, sem):
        both(ref, sem).wait_recv()

    def sent(ref, sem, when=None):
        pending.append((ref, sem, when))

    def finish():
        for ref, sem, when in pending:
            if when is None:
                both(ref, sem).wait_send()
            else:
                @pl.when(when)
                def _():
                    both(ref, sem).wait_send()

    def on_leaf(k, src, dst, ss, rs):
        for n, (dz, dx) in enumerate(far_l):
            at_z, at_x = (z + dz) % nz, (x + dx) % NX
            send(src(at_z, at_x), dst(n), ss, rs, {"leaf": at_z * NX + at_x})

    for h in range(2):
        send(rhs_v.at[:, h], gath.at[h, f], af_ss.at[h, 0], af_rs.at[h, 0], {"front": sib})
        sent(rhs_v.at[:, h], af_ss.at[h, 0])
        for d in far_y:
            up = y + d < ny

            @pl.when(up)
            def _():
                send(
                    rhs_v.at[:, h], gath.at[h, f], a_ss.at[h, d], a_rs.at[h, d], {"front": (y + d) % ny * 2 + c}
                )

            sent(rhs_v.at[:, h], a_ss.at[h, d], up)
    for h in range(2):
        gath[h, f] = rhs_v[:, h]

    loads[1].wait()
    for j in range(ny):
        inv_h[j], inv_l[j] = split2(inv_v[:, 2 * j * ks : 2 * (j + 1) * ks])
    loads[2].wait()
    upd_h[...], upd_l[...] = split2(upd_v[...])
    loads[3].wait()
    low = map_v[...] % width
    onehot[...] = jnp.where(lax.broadcasted_iota(jnp.int32, (width, ku), 0) == low, 1.0, 0.0).astype(BF16)

    def in_block():
        return lax.broadcasted_iota(jnp.int32, (nl, rows, ku), 0) == (map_v[...] // width)[None]

    def solve_step(h, at):
        pair = jnp.concatenate([gath[h, 2 * at + k].reshape(half, ks) for k in range(2)], axis=1)
        return mul3(pair, inv_h[at], inv_l[at], NT)

    def solve(h):
        def step(d):
            wait_recv(gath.at[h, 0], af_rs.at[h, d])
            acc[h] += solve_step(h, (y + ny - d) % ny)

        wait_recv(gath.at[h, 0], af_rs.at[h, 0])
        acc[h] = solve_step(h, y)
        before = None
        for d in near_y:
            low_chip = y >= d

            @pl.when(low_chip)
            def _():
                came = (y + ny - d) % ny * 2 + c
                wait_recv(gath.at[h, came], a_rs.at[h, d])
                send(gath.at[h, came], gath.at[h, came], af_ss.at[h, d], af_rs.at[h, d], {"front": sib})

            sent(gath.at[h, 0], af_ss.at[h, d], low_chip)
            if before is not None:
                @pl.when(y >= before)
                def _():
                    step(before)
            before = d

        @pl.when(y >= before)
        def _():
            step(before)

    def partial_update(h):
        return mul3(acc[h], upd_h[...], upd_l[...], NT).reshape(ny, rows, ku)

    def give_update(h):
        @pl.when(c != h)
        def _():
            b_send[...] = partial_update(h)
            send(b_send, b_pair, s_sem.at[0], r_sem.at[0], {"front": sib})

        @pl.when(c == h)
        def _():
            mine = partial_update(h)
            wait_recv(b_pair, r_sem.at[0])
            b_own[...] = mine + b_pair[...]
            for n, d in enumerate(far_y):
                at = (y + d) % ny
                send(b_own.at[at], b_recv.at[n], s_sem.at[1], r_sem.at[1], {"front": at * 2 + c})

    sent(b_send, s_sem.at[0])
    sent(b_recv, s_sem.at[1])

    def give_columns():
        wait_recv(b_recv, r_sem.at[1])
        update = b_own[y] + jnp.sum(b_recv[...], axis=0)
        mask = in_block()
        parts = [
            jnp.where(mask, jnp.broadcast_to(p.astype(F32)[None], (nl, rows, ku)), 0.0)
            .reshape(nl * rows, ku)
            .astype(BF16)
            for p in split3(update)
        ]
        c_send[...] = (
            mul(parts[0], onehot[...], NT) + (mul(parts[1], onehot[...], NT) + mul(parts[2], onehot[...], NT))
        ).reshape(nl, rows, width)
        on_leaf(2, lambda at_z, at_x: c_send.at[at_z * NX + at_x], lambda n: c_recv.at[n], s_sem.at[2], r_sem.at[2])

    sent(c_recv, s_sem.at[2])

    def give_reduced(h):
        wait_recv(c_recv, r_sem.at[2])
        d_buf[h, y] = rr_v[...] - (c_send[l] + jnp.sum(c_recv[...], axis=0))
        for d in far_y:
            for k in range(2):
                at = (y + d) % ny * 2 + k
                send(d_buf.at[h, y], d_buf.at[h, y], s_sem.at[3], r_sem.at[3 + h], {"front": at})
        send(d_buf.at[h, y], d_buf.at[h, y], s_sem.at[3], r_sem.at[3 + h], {"front": sib})

    sent(c_recv.at[pl.ds(0, nf - 1)], s_sem.at[3])

    def give_forward(h):
        @pl.when(c == h)
        def _():
            wait_recv(d_buf.at[h, pl.ds(0, ny - 1)], r_sem.at[3 + h])

        @pl.when(c != h)
        def _():
            wait_recv(d_buf.at[h], r_sem.at[3 + h])

        part = mul3(d_buf[h].reshape(half, width), rinv_h[...], rinv_l[...], NT)
        for q in range(nq):
            e_send[h, q] = part[:, q * piece : (q + 1) * piece].reshape(ny, rows, piece)
        on_leaf(
            5 + h, lambda at_z, at_x: e_send.at[h, at_x, at_z], lambda n: e_recv.at[h, n], s_sem.at[5 + h], r_sem.at[5 + h]
        )

    def give_solved(h):
        wait_recv(e_recv.at[h], r_sem.at[5 + h])
        f_buf[h, x, z] = e_send[h, x, z] + jnp.sum(e_recv[h], axis=0)
        on_leaf(
            7 + h, lambda at_z, at_x: f_buf.at[h, x, z], lambda n: f_buf.at[h, x, z], s_sem.at[7 + h], r_sem.at[7 + h]
        )

    for h in range(2):
        sent(e_recv.at[h], s_sem.at[5 + h])
        sent(e_recv.at[h], s_sem.at[7 + h])

    def give_backward(h):
        wait_recv(e_recv.at[h], r_sem.at[7 + h])
        root = jnp.concatenate([f_buf[h, q].reshape(half, piece) for q in range(nq)], axis=1)
        g_send[h] = mul3(root, rinv_h[...], rinv_l[...], NN).reshape(ny, rows, width)
        for d in far_y:
            at = (y + d) % ny
            send(g_send.at[h, at], g_recv.at[f], g_ss.at[h, 0], r_sem.at[9], {"front": at * 2 + h})

        @pl.when(c != h)
        def _():
            send(g_send.at[h, y], g_recv.at[f], g_ss.at[h, 1], r_sem.at[9], {"front": sib})

        @pl.when(c == h)
        def _():
            g_recv[f] = g_send[h, y]

        sent(g_send.at[h, pl.ds(0, ny - 1)], g_ss.at[h, 0])
        sent(g_send.at[h, 0], g_ss.at[h, 1], c != h)

    def give_root():
        wait_recv(g_recv.at[pl.ds(0, nf - 1)], r_sem.at[9])
        answer = jnp.sum(g_recv[...], axis=0)
        h_buf[l] = answer
        on_leaf(9, lambda at_z, at_x: h_buf.at[l], lambda n: h_buf.at[l], s_sem.at[9], r_sem.at[10])
        root_out[...] = answer

    sent(h_buf.at[pl.ds(0, nl - 1)], s_sem.at[9])

    def give_picked(h):
        wait_recv(h_buf.at[pl.ds(0, nl - 1)], r_sem.at[10])
        parts = split3(h_buf[...].reshape(nl * rows, width))
        chosen = mul(parts[0], onehot[...], NN) + (mul(parts[1], onehot[...], NN) + mul(parts[2], onehot[...], NN))
        i_buf[h, y] = jnp.sum(jnp.where(in_block(), chosen.reshape(nl, rows, ku), 0.0), axis=0)
        for d in far_y:
            at = (y + d) % ny * 2 + c
            send(i_buf.at[h, y], i_buf.at[h, y], i_ss.at[d], i_rs.at[d], {"front": at})
        send(i_buf.at[h, y], i_buf.at[h, y], if_ss.at[0], if_rs.at[0], {"front": sib})

    for d in range(ny):
        if d:
            sent(i_buf.at[0, 0], i_ss.at[d])
        sent(i_buf.at[0, 0], if_ss.at[d])

    def take_picked(h):
        @pl.when(c == h)
        def _():
            for d in near_y:
                came = (y + ny - d) % ny
                wait_recv(i_buf.at[h, came], i_rs.at[d])
                send(i_buf.at[h, came], i_buf.at[h, came], if_ss.at[d], if_rs.at[d], {"front": sib})

        @pl.when(c != h)
        def _():
            for d in range(ny):
                wait_recv(i_buf.at[h, 0], if_rs.at[d])

    def give_residue(h):
        residue = acc[h] - mul3(i_buf[h].reshape(half, ku), upd_h[...], upd_l[...], NN)
        rh, rl = split2(residue)
        for j in range(ny):
            @pl.when(j <= y)
            def _():
                both_cores = mul(rh, inv_h[j], NN) + (mul(rh, inv_l[j], NN) + mul(rl, inv_h[j], NN))
                left, right = both_cores[:, :ks], both_cores[:, ks:]
                j_send[h, j] = jnp.where(c == 0, right, left)
                j_own[h, j] = jnp.where(c == 0, left, right)

            @pl.when(j > y)
            def _():
                j_send[h, j] = jnp.zeros_like(residue)
        send(j_send.at[h], j_pair.at[h], s_sem.at[10 + h], r_sem.at[11 + h], {"front": sib})

    def give_child(h):
        wait_recv(j_pair.at[h], r_sem.at[11 + h])
        for d in far_y:
            down = y >= d

            @pl.when(down)
            def _():
                at = (y + ny - d) % ny
                j_own[h, at] += j_pair[h, at]
                send(j_own.at[h, at], j_recv.at[h, d - 1], j_ss.at[h, d], j_rs.at[h, d], {"front": at * 2 + c})

        j_own[h, y] += j_pair[h, y]

    for h in range(2):
        sent(j_send.at[h], s_sem.at[10 + h])
        for d in far_y:
            sent(j_own.at[h, 0], j_ss.at[h, d], y >= d)

    def take_child(h):
        for d in near_y:
            up = y + d < ny

            @pl.when(up)
            def _():
                wait_recv(j_recv.at[h, d - 1], j_rs.at[h, d])
                j_own[h, y] += j_recv[h, d - 1]

        child_out[:, h] = j_own[h, y].reshape(ny, rows, ks)

    solve(0)
    give_update(0)
    solve(1)
    give_update(1)
    loads[4].wait()
    rinv_h[...], rinv_l[...] = split2(rinv_v[...])
    loads[5].wait()
    give_columns()

    @pl.when(c == 0)
    def _():
        give_reduced(0)

    @pl.when(c == 1)
    def _():
        give_reduced(1)

    give_forward(0)
    give_forward(1)
    give_solved(0)
    give_solved(1)
    give_backward(0)
    give_backward(1)
    give_root()

    @pl.when(c == 0)
    def _():
        give_picked(0)

    @pl.when(c == 1)
    def _():
        give_picked(1)

    take_picked(0)
    give_residue(0)
    give_child(0)
    take_picked(1)
    give_residue(1)
    give_child(1)
    take_child(0)
    take_child(1)
    finish()


def body(nl, nf, rhs_child, child_inverse, update_block, row_map, rhs_root, root_inverse):
    ny = nf // 2
    frames, ks = rhs_child.shape[1:]
    ku = update_block.shape[1]
    rows, width = rhs_root.shape
    deep = root_inverse.shape[0]
    half = ny * rows
    piece = half * deep // nl // rows
    nq = deep // piece
    vm = pltpu.VMEM
    dma = pltpu.SemaphoreType.DMA
    scratch = [
        vm((ny, 2, rows, ks), F32), vm((ks, nf * ks), F32), vm((ku, ks), F32), vm((deep, width), F32),
        vm((1, ku), jnp.int32), vm((rows, width), F32),
        vm((2, nf, ny, rows, ks), F32), vm((2, half, ks), F32),
        vm((ny, ks, 2 * ks), BF16), vm((ny, ks, 2 * ks), BF16),
        vm((ku, ks), BF16), vm((ku, ks), BF16),
        vm((deep, width), BF16), vm((deep, width), BF16),
        vm((width, ku), BF16),
        vm((ny, rows, ku), F32), vm((ny, rows, ku), F32), vm((ny, rows, ku), F32), vm((ny - 1, rows, ku), F32),
        vm((nl, rows, width), F32), vm((nl - 1, rows, width), F32),
        vm((2, ny, rows, width), F32),
        vm((2, nq, ny, rows, piece), F32), vm((2, nl - 1, rows, piece), F32),
        vm((2, nq, ny, rows, piece), F32),
        vm((2, ny, rows, width), F32), vm((nf, rows, width), F32),
        vm((nl, rows, width), F32),
        vm((2, ny, rows, ku), F32),
        vm((2, ny, half, ks), F32), vm((2, ny, half, ks), F32), vm((2, ny, half, ks), F32),
        vm((2, ny - 1, half, ks), F32),
        dma((6,)), dma((2, ny)), dma((2, ny)), dma((2, ny)), dma((2, ny)),
        dma((ny,)), dma((ny,)), dma((ny,)), dma((ny,)),
        dma((12,)), dma((13,)), dma((2, 2)), dma((2, ny)), dma((2, ny)),
    ]
    child, root = pl.pallas_call(
        functools.partial(kernel, nl, nf),
        out_shape=(
            jax.ShapeDtypeStruct((ny, 2, rows, ks), F32),
            jax.ShapeDtypeStruct((rows, width), F32),
        ),
        in_specs=[pl.BlockSpec(memory_space=pl.ANY)] * 6,
        out_specs=(pl.BlockSpec(memory_space=pltpu.VMEM),) * 2,
        scratch_shapes=scratch,
        compiler_params=pltpu.CompilerParams(
            collective_id=0, has_side_effects=True, vmem_limit_bytes=56 * 1024 * 1024
        ),
    )(
        rhs_child.reshape(ny, 2, rows, ks), child_inverse[0], update_block[0], row_map, rhs_root, root_inverse
    )
    return child.reshape(1, frames, ks), root


def solution(mesh):
    placed = (
        P("leaf", None, "front"),
        P("leaf", "front", None),
        P("leaf", None, "front"),
        P("leaf", None),
        P("front", "leaf"),
        P("front", "leaf"),
    )
    return jax.shard_map(
        functools.partial(body, mesh.shape["leaf"], mesh.shape["front"]),
        mesh=mesh,
        in_specs=placed,
        out_specs=(P("leaf", None, "front"), P("front", "leaf")),
        check_vma=False,
    )
```

time: 763 us -> 106 us (0.14)
  waiting for transfers between devices: 670 us -> 0 us
  Pallas kernels: 0 us -> 103 us
  blocking collectives: 41.3 us -> 0 us
  between operations: 14.2 us -> 0.65 us
  local copies, waits for them, and re-layouts: 15.1 us -> 2.08 us
  matrix products: 11.1 us -> 0 us
  other arithmetic: 9.62 us -> 0 us
    reduce_scatter x3 -> x0, waiting for transfers between devices: 334 us -> none  [the longest x1 214 us: body(): lax.psum_scatter(spread_rows, 'leaf', scatter_dimension=1, tiled=True)]
    psum x1 -> x0, waiting for transfers between devices: 146 us -> none  [body(): solved_root = lax.psum(partial_value, 'leaf')]
    all_gather x2 -> x0, waiting for transfers between devices: 133 us -> none  [the longest x1 85.4 us: body(): complete = lax.all_gather(columns, 'leaf', axis=1, tiled=True)]
    pallas_call x0 -> x1, Pallas kernels: none -> 103 us  [body(): pl.pallas_call(functools.partial(kernel, nl, nf), out_shape=(jax.ShapeDty...]
    unnamed x8 -> x0, waiting for transfers between devices: 56.3 us -> none
    all_gather x2 -> x0, blocking collectives: 41.3 us -> none  [the longest x1 23 us: body(): lax.all_gather(reduced, 'front', axis=0, tiled=True)]
    dot_general x5 -> x0, matrix products: 8.71 us -> none  [the longest x3 5.15 us: product(): jnp.dot(left, right, precision=lax.Precision.HIGHEST, preferred_element_t...]
    scatter-add x1 -> x0, other arithmetic: 8.21 us -> none  [body(): jnp.zeros((frame_share, P_SIZE), jnp.float32).at[:, targets].add(update)]
  transfers between devices with their start and end apart: 7 -> 0, of which waited for: 7 -> 0; matrix products, arithmetic and copies ran while one was open for 0% -> 0% of each run, Pallas kernels for 0% -> 0%
where the time goes in v2:
time: 106 us
  Pallas kernels  103 us (97%)
  local copies, waits for them, and re-layouts  2.08 us (2%)
    pallas_call x1, Pallas kernels, body(): pl.pallas_call(functools.partial(kernel, nl, nf), out_shape=(jax.ShapeDty...  103 us

profile of v2, /device:TPU:1, one launch (start us, length us, event | category | flops | bytes accessed | tf_op | source)
XLA Modules:
  0.0 105.9 jit_solution(16364276837648380806)
XLA Ops:
  0.6 103.2 %shard_map.77 = (f32[8,2,8,128]{3,2,1,0:T(8,128)}, f32[8,256]{1,0:T(8,128)}) custom-call(f32[8,2,8,128]{3,2,1,0:T(8,128)} %bitcast.6, f32[128,2048]{1,0:T(8,128)} %bitcast.4, f32[1024,128]{1,0:T(8,128)} %bitcast.5, s32[1,1024]{1,0:T(1,128)} %rmap.1, f32[8,256]{1,0:T(8,128)} %rhs_r.1, f32[512,256]{1,0:T(8,128)} %rinv.1), custom_call_target="tpu_custom_call" | custom-call | tf_op jit(solution)/shard_map/pallas_call | solution.py:435
  103.8 0.0 copy-start
  103.8 1.5 %copy.10 = f32[1,128,128]{2,1,0:T(8,128)} copy(f32[1,128,128]{2,1,0:T(8,128)} %bitcast.7) | data formatting | bytes 131072
  105.3 0.0 copy-done
  105.3 0.6 copy.11
Async XLA Ops:
  103.8 1.5 %copy-start = (f32[8,256]{1,0:T(8,128)S(1)}, f32[8,256]{1,0:T(8,128)}, u32[]{:S(2)}) copy-start(f32[8,256]{1,0:T(8,128)} %get-tuple-element.9) | copy-start | bytes 24580

commit v3 on v0

v3 whole, which is shorter than its diff:
```python
import functools

import jax
import jax.numpy as jnp
from jax import lax
from jax.experimental import pallas as pl
from jax.experimental.pallas import tpu as pltpu
from jax.sharding import PartitionSpec as P

NX = 4
MESH = pl.DeviceIdType.MESH
F32 = jnp.float32
BF16 = jnp.bfloat16
NN = (((1,), (0,)), ((), ()))
NT = (((1,), (1,)), ((), ()))


def split2(x):
    hi = x.astype(BF16)
    return hi, (x - hi.astype(F32)).astype(BF16)


def mul(a, b, dims):
    return lax.dot_general(a, b, dims, preferred_element_type=F32)


def mul3(a, bh, bl, dims):
    ah, al = split2(a)
    n = a.shape[0]
    both = mul(jnp.concatenate([ah, al], axis=0), bh, dims)
    return both[:n] + (both[n:] + mul(ah, bl, dims))


def ring_hops(d, n):
    return min(d, n - d)


def kernel(
    nl, nf,
    rhs_c, inv, upd, rmap, rhs_r, rinv,
    child_out, root_out,
    rhs_v, inv_v, upd_v, rinv_v, map_v, rr_v,
    gath, acc, inv_h, inv_l, upd_h, upd_l, rinv_h, rinv_l, onehot,
    b_send, b_recv, c_send, c_recv, d_buf, e_send, e_recv, f_buf,
    g_send, g_recv, h_buf, i_buf, j_send, j_recv,
    in_sem, p_ss, p_rs, a_ss, a_rs, s_sem, r_sem, j_ss, j_rs,
):
    ny = nf // 2
    nz = nl // NX
    l = lax.axis_index("leaf")
    f = lax.axis_index("front")
    y, c = f // 2, f % 2
    z, x = l // NX, l % NX
    sib = y * 2 + (1 - c)
    rows, width = rr_v.shape
    ks, ku = rhs_v.shape[-1], upd_v.shape[1]
    half = ny * rows
    nq = e_send.shape[0]

    far_y = sorted(range(1, ny), key=lambda d: -ring_hops(d, ny))
    near_y = sorted(range(1, ny), key=lambda d: ring_hops(d, ny))
    relayed_y = [d for d in (3, 4) if d < ny - 2]
    direct_y = [d for d in (2, 5, 6, 1, 7) if d < ny and d not in relayed_y] if ny > 4 else far_y
    arrive_y = [d for d in (2, 1, 7, 6, 5, 3, 4) if d < ny]
    far_l = sorted(
        [(dz, dx) for dz in range(nz) for dx in range(NX) if dz or dx],
        key=lambda d: -(ring_hops(d[0], nz) + ring_hops(d[1], NX)),
    )

    loads = [
        pltpu.make_async_copy(src, dst, in_sem.at[k])
        for k, (src, dst) in enumerate(
            [
                (rhs_c, rhs_v), (inv, inv_v.at[c]), (upd, upd_v.at[c]), (rmap, map_v),
                (rinv, rinv_v.at[c]), (rhs_r, rr_v),
            ]
        )
    ]
    for load in loads:
        load.start()
    barrier = pltpu.get_barrier_semaphore()
    for dz, dx in far_l:
        at = (z + dz) % nz * NX + (x + dx) % NX
        pl.semaphore_signal(barrier, inc=1, device_id={"leaf": at}, device_id_type=MESH)
    for d in far_y:
        for k in range(2):
            pl.semaphore_signal(barrier, inc=1, device_id={"front": (y + d) % ny * 2 + k}, device_id_type=MESH)
    pl.semaphore_signal(barrier, inc=1, device_id={"front": sib}, device_id_type=MESH)
    loads[0].wait()
    pl.semaphore_wait(barrier, nf + nl - 2)

    pending = []

    def send(src, dst, ss, rs, where):
        pltpu.make_async_remote_copy(
            src_ref=src, dst_ref=dst, send_sem=ss, recv_sem=rs, device_id=where, device_id_type=MESH
        ).start()

    def both(ref, sem):
        return pltpu.make_async_remote_copy(
            src_ref=ref, dst_ref=ref, send_sem=sem, recv_sem=sem, device_id={"front": sib}, device_id_type=MESH
        )

    def wait_recv(ref, sem):
        both(ref, sem).wait_recv()

    def sent(ref, sem, when=None):
        pending.append((ref, sem, when))

    def finish():
        for ref, sem, when in pending:
            if when is None:
                both(ref, sem).wait_send()
            else:
                @pl.when(when)
                def _():
                    both(ref, sem).wait_send()

    def on_leaf(k, src, dst, ref):
        for n, (dz, dx) in enumerate(far_l):
            at_z, at_x = (z + dz) % nz, (x + dx) % NX
            send(src(at_z, at_x), dst(n), s_sem.at[k], r_sem.at[k], {"leaf": at_z * NX + at_x})
        sent(ref, s_sem.at[k])

    def on_y(k, src, dst, ref):
        for n, d in enumerate(far_y):
            at = (y + d) % ny
            send(src(at), dst(n), s_sem.at[k], r_sem.at[k], {"front": at * 2 + c})
        sent(ref, s_sem.at[k])

    send(rhs_v.at[:, 1 - c], gath.at[f], p_ss.at[0], p_rs.at[0], {"front": sib})
    sent(rhs_v.at[:, 0], p_ss.at[0])
    for h in range(2):
        for d in direct_y:
            up = y + d < ny

            @pl.when(up)
            def _():
                send(rhs_v.at[:, h], gath.at[f], a_ss.at[h, d], a_rs.at[d], {"front": (y + d) % ny * 2 + h})

            sent(rhs_v.at[:, h], a_ss.at[h, d], up)
    for n, (src, dst) in enumerate([(inv, inv_v.at[c]), (upd, upd_v.at[c]), (rinv, rinv_v.at[c])]):
        send(src, dst, p_ss.at[n + 1], p_rs.at[n + 1], {"front": sib})
        sent(dst, p_ss.at[n + 1])
    gath[f] = rhs_v[:, c]

    loads[3].wait()
    low = map_v[...] % width
    onehot[...] = jnp.where(lax.broadcasted_iota(jnp.int32, (width, ku), 0) == low, 1.0, 0.0).astype(BF16)
    loads[1].wait()
    wait_recv(inv_v.at[0], p_rs.at[1])
    for j in range(ny):
        for k in range(2):
            inv_h[j, k * ks : (k + 1) * ks], inv_l[j, k * ks : (k + 1) * ks] = split2(
                inv_v[k, :, 2 * j * ks : 2 * (j + 1) * ks]
            )
    if relayed_y:
        @pl.when(y >= 2)
        def _():
            pair = gath.at[pl.ds((y + ny - 2) % ny * 2, 2)]
            wait_recv(pair, a_rs.at[2])
            for d in relayed_y:
                @pl.when(y + d - 2 < ny)
                def _():
                    send(pair, pair, a_ss.at[0, d], a_rs.at[d], {"front": (y + d - 2) % ny * 2 + c})

        for d in relayed_y:
            sent(gath.at[pl.ds(0, 2)], a_ss.at[0, d], (y >= 2) & (y + d - 2 < ny))
    loads[2].wait()
    wait_recv(upd_v.at[0], p_rs.at[2])
    for k in range(2):
        upd_h[:, k * ks : (k + 1) * ks], upd_l[:, k * ks : (k + 1) * ks] = split2(upd_v[k])

    def in_block():
        return lax.broadcasted_iota(jnp.int32, (nl, rows, ku), 0) == (map_v[...] // width)[None]

    def solve_step(at):
        pair = jnp.concatenate([gath[2 * at + k].reshape(half, ks) for k in range(2)], axis=1)
        return mul3(pair, inv_h[at], inv_l[at], NT)

    wait_recv(gath.at[0], p_rs.at[0])
    acc[...] = solve_step(y)
    for d in arrive_y:
        @pl.when(y >= d)
        def _():
            if d != 2 or not relayed_y:
                wait_recv(gath.at[pl.ds(0, 2)], a_rs.at[d])
            acc[...] += solve_step((y + ny - d) % ny)

    b_send[...] = mul3(acc[...], upd_h[...], upd_l[...], NT).reshape(ny, rows, ku)
    on_y(0, lambda at: b_send.at[at], lambda n: b_recv.at[n], b_recv)
    loads[4].wait()
    wait_recv(rinv_v.at[0], p_rs.at[3])
    deep = rinv_v.shape[1]
    for k in range(2):
        rinv_h[k * deep : (k + 1) * deep], rinv_l[k * deep : (k + 1) * deep] = split2(rinv_v[k])
    loads[5].wait()
    wait_recv(b_recv, r_sem.at[0])
    update = b_send[y] + jnp.sum(b_recv[...], axis=0)

    mask = in_block()
    parts = [
        jnp.where(mask, jnp.broadcast_to(p.astype(F32)[None], (nl, rows, ku)), 0.0).reshape(nl * rows, ku).astype(BF16)
        for p in split2(update)
    ]
    c_send[...] = (mul(parts[0], onehot[...], NT) + mul(parts[1], onehot[...], NT)).reshape(nl, rows, width)
    on_leaf(1, lambda at_z, at_x: c_send.at[at_z * NX + at_x], lambda n: c_recv.at[n], c_recv)
    wait_recv(c_recv, r_sem.at[1])

    d_buf[y] = rr_v[...] - (c_send[l] + jnp.sum(c_recv[...], axis=0))
    on_y(2, lambda at: d_buf.at[y], lambda n: d_buf.at[y], d_buf.at[pl.ds(0, ny - 1)])
    wait_recv(d_buf.at[pl.ds(0, ny - 1)], r_sem.at[2])

    part = mul3(d_buf[...].reshape(half, width), rinv_h[...], rinv_l[...], NT)
    piece = e_send.shape[-1]
    for q in range(nq):
        e_send[q] = part[:, q * piece : (q + 1) * piece].reshape(ny, rows, piece)
    on_leaf(3, lambda at_z, at_x: e_send.at[at_x, at_z], lambda n: e_recv.at[n], e_recv)
    wait_recv(e_recv, r_sem.at[3])
    f_buf[x, z] = e_send[x, z] + jnp.sum(e_recv[...], axis=0)

    on_leaf(4, lambda at_z, at_x: f_buf.at[x, z], lambda n: f_buf.at[x, z], e_recv)
    wait_recv(e_recv, r_sem.at[4])

    root = jnp.concatenate([f_buf[q].reshape(half, piece) for q in range(nq)], axis=1)
    g_send[...] = mul3(root, rinv_h[...], rinv_l[...], NN).reshape(ny, rows, width)
    on_y(5, lambda at: g_send.at[at], lambda n: g_recv.at[n], g_recv)
    wait_recv(g_recv, r_sem.at[5])
    answer = g_send[y] + jnp.sum(g_recv[...], axis=0)

    h_buf[l] = answer
    on_leaf(6, lambda at_z, at_x: h_buf.at[l], lambda n: h_buf.at[l], h_buf.at[pl.ds(0, nl - 1)])
    root_out[...] = answer
    wait_recv(h_buf.at[pl.ds(0, nl - 1)], r_sem.at[6])
    columns = jnp.concatenate(split2(h_buf[...].reshape(nl * rows, width)), axis=0)
    chosen = mul(columns, onehot[...], NN)
    chosen = (chosen[: nl * rows] + chosen[nl * rows :]).reshape(nl, rows, ku)

    i_buf[y] = jnp.sum(jnp.where(in_block(), chosen, 0.0), axis=0)
    on_y(7, lambda at: i_buf.at[y], lambda n: i_buf.at[y], i_buf.at[pl.ds(0, ny - 1)])
    wait_recv(i_buf.at[pl.ds(0, ny - 1)], r_sem.at[7])
    residue = acc[...] - mul3(i_buf[...].reshape(half, ku), upd_h[...], upd_l[...], NN)
    acc[...] = residue

    def back(d):
        at = (y + ny - d) % ny
        wide = mul3(acc[...], inv_h[at], inv_l[at], NN)
        for k in range(2):
            j_send[d, k] = wide[:, k * ks : (k + 1) * ks]
        return at

    for d in relayed_y[::-1]:
        @pl.when(y >= d)
        def _():
            back(d)
            send(j_send.at[d], j_recv.at[d], j_ss.at[d, 0], j_rs.at[d, 0], {"front": (y + ny + 2 - d) % ny * 2 + c})

        sent(j_send.at[0], j_ss.at[d, 0], y >= d)

    def give_child(d):
        down = y >= d

        @pl.when(down)
        def _():
            at = (y + ny - d) % ny
            for k in range(2):
                send(j_send.at[d, k], j_recv.at[d, c], j_ss.at[d, k], j_rs.at[d, c], {"front": at * 2 + k})

        for k in range(2):
            sent(j_send.at[0, 0], j_ss.at[d, k], down)

    for d in direct_y:
        @pl.when(y >= d)
        def _():
            back(d)

        if d != 2 or not relayed_y:
            give_child(d)
    if relayed_y:
        for d in relayed_y:
            @pl.when((y >= 2) & (y + d - 2 < ny))
            def _():
                wait_recv(j_recv.at[d], j_rs.at[d, 0])
                j_send[2] += j_recv[d]

        give_child(2)
    back(0)
    send(j_send.at[0, 1 - c], j_recv.at[0, c], j_ss.at[0, 0], j_rs.at[0, c], {"front": sib})
    sent(j_send.at[0, 0], j_ss.at[0, 0])
    j_recv[0, c] = j_send[0, c]
    wait_recv(j_recv.at[0, 0], j_rs.at[0, 1 - c])
    for d in arrive_y[1:] + arrive_y[:1]:
        if d in relayed_y:
            continue

        @pl.when(y + d < ny)
        def _():
            for h in range(2):
                wait_recv(j_recv.at[d, h], j_rs.at[d, h])
                j_recv[0, h] += j_recv[d, h]

    for h in range(2):
        child_out[:, h] = j_recv[0, h].reshape(ny, rows, ks)
    finish()


def body(nl, nf, rhs_child, child_inverse, update_block, row_map, rhs_root, root_inverse):
    ny = nf // 2
    frames, ks = rhs_child.shape[1:]
    ku = update_block.shape[1]
    rows, width = rhs_root.shape
    deep = root_inverse.shape[0]
    half = ny * rows
    piece = half * 2 * deep // nl // rows
    nq = 2 * deep // piece
    vm = pltpu.VMEM
    dma = pltpu.SemaphoreType.DMA
    scratch = [
        vm((ny, 2, rows, ks), F32), vm((2, ks, nf * ks), F32), vm((2, ku, ks), F32), vm((2, deep, width), F32),
        vm((1, ku), jnp.int32), vm((rows, width), F32),
        vm((nf, ny, rows, ks), F32), vm((half, 2 * ks), F32),
        vm((ny, 2 * ks, 2 * ks), BF16), vm((ny, 2 * ks, 2 * ks), BF16),
        vm((ku, 2 * ks), BF16), vm((ku, 2 * ks), BF16),
        vm((2 * deep, width), BF16), vm((2 * deep, width), BF16),
        vm((width, ku), BF16),
        vm((ny, rows, ku), F32), vm((ny - 1, rows, ku), F32),
        vm((nl, rows, width), F32), vm((nl - 1, rows, width), F32),
        vm((ny, rows, width), F32),
        vm((nq, ny, rows, piece), F32), vm((nl - 1, rows, piece), F32),
        vm((nq, ny, rows, piece), F32),
        vm((ny, rows, width), F32), vm((ny - 1, rows, width), F32),
        vm((nl, rows, width), F32),
        vm((ny, rows, ku), F32),
        vm((ny, 2, half, ks), F32), vm((ny, 2, half, ks), F32),
        dma((6,)), dma((4,)), dma((4,)), dma((2, ny)), dma((ny,)),
        dma((8,)), dma((8,)), dma((ny, 2)), dma((ny, 2)),
    ]
    child, root = pl.pallas_call(
        functools.partial(kernel, nl, nf),
        out_shape=(
            jax.ShapeDtypeStruct((ny, 2, rows, ks), F32),
            jax.ShapeDtypeStruct((rows, width), F32),
        ),
        in_specs=[pl.BlockSpec(memory_space=pl.ANY)] * 6,
        out_specs=(pl.BlockSpec(memory_space=pltpu.VMEM),) * 2,
        scratch_shapes=scratch,
        compiler_params=pltpu.CompilerParams(
            collective_id=0, has_side_effects=True, vmem_limit_bytes=56 * 1024 * 1024
        ),
    )(
        rhs_child.reshape(ny, 2, rows, ks), child_inverse[0], update_block[0], row_map, rhs_root, root_inverse
    )
    return child.reshape(1, frames, ks), root


def solution(mesh):
    placed = (
        P("leaf", None, "front"),
        P("leaf", "front", None),
        P("leaf", None, "front"),
        P("leaf", None),
        P("front", "leaf"),
        P("front", "leaf"),
    )
    return jax.shard_map(
        functools.partial(body, mesh.shape["leaf"], mesh.shape["front"]),
        mesh=mesh,
        in_specs=placed,
        out_specs=(P("leaf", None, "front"), P("front", "leaf")),
        check_vma=False,
    )
```

time: 763 us -> 101 us (0.13)
  waiting for transfers between devices: 670 us -> 0 us
  Pallas kernels: 0 us -> 97.6 us
  blocking collectives: 41.3 us -> 0 us
  between operations: 14.2 us -> 0.65 us
  local copies, waits for them, and re-layouts: 15.1 us -> 2.08 us
  matrix products: 11.1 us -> 0 us
  other arithmetic: 9.62 us -> 0 us
    reduce_scatter x3 -> x0, waiting for transfers between devices: 334 us -> none  [the longest x1 214 us: body(): lax.psum_scatter(spread_rows, 'leaf', scatter_dimension=1, tiled=True)]
    psum x1 -> x0, waiting for transfers between devices: 146 us -> none  [body(): solved_root = lax.psum(partial_value, 'leaf')]
    all_gather x2 -> x0, waiting for transfers between devices: 133 us -> none  [the longest x1 85.4 us: body(): complete = lax.all_gather(columns, 'leaf', axis=1, tiled=True)]
    pallas_call x0 -> x1, Pallas kernels: none -> 97.6 us  [body(): pl.pallas_call(functools.partial(kernel, nl, nf), out_shape=(jax.ShapeDty...]
    unnamed x8 -> x0, waiting for transfers between devices: 56.3 us -> none
    all_gather x2 -> x0, blocking collectives: 41.3 us -> none  [the longest x1 23 us: body(): lax.all_gather(reduced, 'front', axis=0, tiled=True)]
    dot_general x5 -> x0, matrix products: 8.71 us -> none  [the longest x3 5.15 us: product(): jnp.dot(left, right, precision=lax.Precision.HIGHEST, preferred_element_t...]
    scatter-add x1 -> x0, other arithmetic: 8.21 us -> none  [body(): jnp.zeros((frame_share, P_SIZE), jnp.float32).at[:, targets].add(update)]
  transfers between devices with their start and end apart: 7 -> 0, of which waited for: 7 -> 0; matrix products, arithmetic and copies ran while one was open for 0% -> 0% of each run, Pallas kernels for 0% -> 0%
where the time goes in v3:
time: 101 us; the launch traced here: 100 us
  Pallas kernels  97.6 us (97%)
  local copies, waits for them, and re-layouts  2.08 us (2%)
    pallas_call x1, Pallas kernels, body(): pl.pallas_call(functools.partial(kernel, nl, nf), out_shape=(jax.ShapeDty...  97.6 us
    unnamed x4, local copies, waits for them, and re-layouts  2.08 us

profile of v3, /device:TPU:1, one launch (start us, length us, event | category | flops | bytes accessed | tf_op | source)
XLA Modules:
  0.0 100.3 jit_solution(8850997742733584525)
XLA Ops:
  0.6 97.6 %shard_map.77 = (f32[8,2,8,128]{3,2,1,0:T(8,128)}, f32[8,256]{1,0:T(8,128)}) custom-call(f32[8,2,8,128]{3,2,1,0:T(8,128)} %bitcast.6, f32[128,2048]{1,0:T(8,128)} %bitcast.4, f32[1024,128]{1,0:T(8,128)} %bitcast.5, s32[1,1024]{1,0:T(1,128)} %rmap.1, f32[8,256]{1,0:T(8,128)} %rhs_r.1, f32[512,256]{1,0:T(8,128)} %rinv.1), custom_call_target="tpu_custom_call" | custom-call | tf_op jit(solution)/shard_map/pallas_call | solution.py:338
  98.2 0.0 copy-start
  98.2 1.5 %copy.10 = f32[1,128,128]{2,1,0:T(8,128)} copy(f32[1,128,128]{2,1,0:T(8,128)} %bitcast.7) | data formatting | bytes 131072
  99.7 0.0 copy-done
  99.7 0.6 copy.11
Async XLA Ops:
  98.2 1.5 %copy-start = (f32[8,256]{1,0:T(8,128)S(1)}, f32[8,256]{1,0:T(8,128)}, u32[]{:S(2)}) copy-start(f32[8,256]{1,0:T(8,128)} %get-tuple-element.9) | copy-start | bytes 24580

commit v4 on v3

--- a/solution.py
+++ b/solution.py
@@ -122,6 +122,20 @@
             send(src(at_z, at_x), dst(n), s_sem.at[k], r_sem.at[k], {"leaf": at_z * NX + at_x})
         sent(ref, s_sem.at[k])
 
+    def by_column(k, make, src, dst):
+        count = 0
+        for dx in sorted(range(NX), key=lambda d: -ring_hops(d, NX)):
+            at_x = (x + dx) % NX
+            make(at_x)
+            for dz in sorted(range(nz), key=lambda d: -ring_hops(d, nz)):
+                if dz or dx:
+                    at_z = (z + dz) % nz
+                    send(
+                        src.at[at_x, at_z], dst.at[count], s_sem.at[k], r_sem.at[k], {"leaf": at_z * NX + at_x}
+                    )
+                    count += 1
+        sent(dst, s_sem.at[k])
+
     def on_y(k, src, dst, ref):
         for n, d in enumerate(far_y):
             at = (y + d) % ny
@@ -198,24 +212,30 @@
     wait_recv(b_recv, r_sem.at[0])
     update = b_send[y] + jnp.sum(b_recv[...], axis=0)
 
-    mask = in_block()
-    parts = [
-        jnp.where(mask, jnp.broadcast_to(p.astype(F32)[None], (nl, rows, ku)), 0.0).reshape(nl * rows, ku).astype(BF16)
-        for p in split2(update)
-    ]
-    c_send[...] = (mul(parts[0], onehot[...], NT) + mul(parts[1], onehot[...], NT)).reshape(nl, rows, width)
-    on_leaf(1, lambda at_z, at_x: c_send.at[at_z * NX + at_x], lambda n: c_recv.at[n], c_recv)
+    high = map_v[...] // width
+    values = [jnp.broadcast_to(p.astype(F32)[None], (nz, rows, ku)) for p in split2(update)]
+
+    def spread(at_x):
+        mask = lax.broadcasted_iota(jnp.int32, (nz, rows, ku), 0) * NX + at_x == high[None]
+        placed = [jnp.where(mask, v, 0.0).reshape(nz * rows, ku).astype(BF16) for v in values]
+        wide = mul(jnp.concatenate(placed, axis=0), onehot[...], NT)
+        c_send[at_x] = (wide[: nz * rows] + wide[nz * rows :]).reshape(nz, rows, width)
+
+    by_column(1, spread, c_send, c_recv)
     wait_recv(c_recv, r_sem.at[1])
 
-    d_buf[y] = rr_v[...] - (c_send[l] + jnp.sum(c_recv[...], axis=0))
+    d_buf[y] = rr_v[...] - (c_send[x, z] + jnp.sum(c_recv[...], axis=0))
     on_y(2, lambda at: d_buf.at[y], lambda n: d_buf.at[y], d_buf.at[pl.ds(0, ny - 1)])
     wait_recv(d_buf.at[pl.ds(0, ny - 1)], r_sem.at[2])
 
-    part = mul3(d_buf[...].reshape(half, width), rinv_h[...], rinv_l[...], NT)
     piece = e_send.shape[-1]
-    for q in range(nq):
-        e_send[q] = part[:, q * piece : (q + 1) * piece].reshape(ny, rows, piece)
-    on_leaf(3, lambda at_z, at_x: e_send.at[at_x, at_z], lambda n: e_recv.at[n], e_recv)
+    ahead = d_buf[...].reshape(half, width)
+
+    def forward(at_x):
+        span = pl.ds(pl.multiple_of(at_x * piece, piece), piece)
+        e_send[at_x] = mul3(ahead, rinv_h[span], rinv_l[span], NT).reshape(ny, rows, piece)
+
+    by_column(3, forward, e_send, e_recv)
     wait_recv(e_recv, r_sem.at[3])
     f_buf[x, z] = e_send[x, z] + jnp.sum(e_recv[...], axis=0)
 
@@ -324,7 +344,7 @@
         vm((2 * deep, width), BF16), vm((2 * deep, width), BF16),
         vm((width, ku), BF16),
         vm((ny, rows, ku), F32), vm((ny - 1, rows, ku), F32),
-        vm((nl, rows, width), F32), vm((nl - 1, rows, width), F32),
+        vm((NX, nl // NX, rows, width), F32), vm((nl - 1, rows, width), F32),
         vm((ny, rows, width), F32),
         vm((nq, ny, rows, piece), F32), vm((nl - 1, rows, piece), F32),
         vm((nq, ny, rows, piece), F32),

time: 101 us -> 98.2 us (0.972)
  Pallas kernels: 97.6 us -> 95.1 us
    pallas_call x1, Pallas kernels: 97.6 us -> 95.1 us  [body(): pl.pallas_call(functools.partial(kernel, nl, nf), out_shape=(jax.ShapeDty...]
where the time goes in v4:
time: 98.2 us; the launch traced here: 97.8 us
  Pallas kernels  95.1 us (97%)
  local copies, waits for them, and re-layouts  2.08 us (2%)
    pallas_call x1, Pallas kernels, body(): pl.pallas_call(functools.partial(kernel, nl, nf), out_shape=(jax.ShapeDty...  95.1 us
    unnamed x4, local copies, waits for them, and re-layouts  2.08 us

profile of v4, /device:TPU:1, one launch (start us, length us, event | category | flops | bytes accessed | tf_op | source)
XLA Modules:
  0.0 97.8 jit_solution(3603791288959090778)
XLA Ops:
  0.6 95.1 %shard_map.77 = (f32[8,2,8,128]{3,2,1,0:T(8,128)}, f32[8,256]{1,0:T(8,128)}) custom-call(f32[8,2,8,128]{3,2,1,0:T(8,128)} %bitcast.6, f32[128,2048]{1,0:T(8,128)} %bitcast.4, f32[1024,128]{1,0:T(8,128)} %bitcast.5, s32[1,1024]{1,0:T(1,128)} %rmap.1, f32[8,256]{1,0:T(8,128)} %rhs_r.1, f32[512,256]{1,0:T(8,128)} %rinv.1), custom_call_target="tpu_custom_call" | custom-call | tf_op jit(solution)/shard_map/pallas_call | solution.py:358
  95.7 0.0 copy-start
  95.7 1.5 %copy.10 = f32[1,128,128]{2,1,0:T(8,128)} copy(f32[1,128,128]{2,1,0:T(8,128)} %bitcast.7) | data formatting | bytes 131072
  97.2 0.0 copy-done
  97.2 0.6 copy.11
Async XLA Ops:
  95.7 1.5 %copy-start = (f32[8,256]{1,0:T(8,128)S(1)}, f32[8,256]{1,0:T(8,128)}, u32[]{:S(2)}) copy-start(f32[8,256]{1,0:T(8,128)} %get-tuple-element.9) | copy-start | bytes 24580

commit v5 on v4

--- a/solution.py
+++ b/solution.py
@@ -54,7 +54,7 @@
     sib = y * 2 + (1 - c)
     rows, width = rr_v.shape
     ks, ku = rhs_v.shape[-1], upd_v.shape[1]
-    half = ny * rows
+    half, kh = ny * rows, ku // 2
     nq = e_send.shape[0]
 
     far_y = sorted(range(1, ny), key=lambda d: -ring_hops(d, ny))
@@ -185,8 +185,9 @@
     for k in range(2):
         upd_h[:, k * ks : (k + 1) * ks], upd_l[:, k * ks : (k + 1) * ks] = split2(upd_v[k])
 
-    def in_block():
-        return lax.broadcasted_iota(jnp.int32, (nl, rows, ku), 0) == (map_v[...] // width)[None]
+    def in_block(part):
+        high = map_v[:, part] // width
+        return lax.broadcasted_iota(jnp.int32, (nl, rows, high.shape[1]), 0) == high[None]
 
     def solve_step(at):
         pair = jnp.concatenate([gath[2 * at + k].reshape(half, ks) for k in range(2)], axis=1)
@@ -253,13 +254,18 @@
     root_out[...] = answer
     wait_recv(h_buf.at[pl.ds(0, nl - 1)], r_sem.at[6])
     columns = jnp.concatenate(split2(h_buf[...].reshape(nl * rows, width)), axis=0)
-    chosen = mul(columns, onehot[...], NN)
-    chosen = (chosen[: nl * rows] + chosen[nl * rows :]).reshape(nl, rows, ku)
-
-    i_buf[y] = jnp.sum(jnp.where(in_block(), chosen, 0.0), axis=0)
-    on_y(7, lambda at: i_buf.at[y], lambda n: i_buf.at[y], i_buf.at[pl.ds(0, ny - 1)])
-    wait_recv(i_buf.at[pl.ds(0, ny - 1)], r_sem.at[7])
-    residue = acc[...] - mul3(i_buf[...].reshape(half, ku), upd_h[...], upd_l[...], NN)
+
+    for p in range(2):
+        part = slice(p * kh, (p + 1) * kh)
+        chosen = mul(columns, onehot[:, part], NN)
+        chosen = (chosen[: nl * rows] + chosen[nl * rows :]).reshape(nl, rows, kh)
+        i_buf[p, y] = jnp.sum(jnp.where(in_block(part), chosen, 0.0), axis=0)
+        on_y(7 + p, lambda at: i_buf.at[p, y], lambda n: i_buf.at[p, y], i_buf.at[p, pl.ds(0, ny - 1)])
+    residue = acc[...]
+    for p in range(2):
+        part = slice(p * kh, (p + 1) * kh)
+        wait_recv(i_buf.at[p, pl.ds(0, ny - 1)], r_sem.at[7 + p])
+        residue -= mul3(i_buf[p].reshape(half, kh), upd_h[part], upd_l[part], NN)
     acc[...] = residue
 
     def back(d):
@@ -350,10 +356,10 @@
         vm((nq, ny, rows, piece), F32),
         vm((ny, rows, width), F32), vm((ny - 1, rows, width), F32),
         vm((nl, rows, width), F32),
-        vm((ny, rows, ku), F32),
+        vm((2, ny, rows, ku // 2), F32),
         vm((ny, 2, half, ks), F32), vm((ny, 2, half, ks), F32),
         dma((6,)), dma((4,)), dma((4,)), dma((2, ny)), dma((ny,)),
-        dma((8,)), dma((8,)), dma((ny, 2)), dma((ny, 2)),
+        dma((9,)), dma((9,)), dma((ny, 2)), dma((ny, 2)),
     ]
     child, root = pl.pallas_call(
         functools.partial(kernel, nl, nf),

time: 98.2 us -> 98.1 us (level)
  no operation moved by 1% of the time
where the time goes in v5:
time: 98.1 us; the launch traced here: 97.9 us
  Pallas kernels  95.1 us (97%)
  local copies, waits for them, and re-layouts  2.08 us (2%)
    pallas_call x1, Pallas kernels, body(): pl.pallas_call(functools.partial(kernel, nl, nf), out_shape=(jax.ShapeDty...  95.1 us
    unnamed x4, local copies, waits for them, and re-layouts  2.08 us

profile of v5, /device:TPU:1, one launch (start us, length us, event | category | flops | bytes accessed | tf_op | source)
XLA Modules:
  0.0 97.9 jit_solution(7110853291176714038)
XLA Ops:
  0.6 95.1 %shard_map.77 = (f32[8,2,8,128]{3,2,1,0:T(8,128)}, f32[8,256]{1,0:T(8,128)}) custom-call(f32[8,2,8,128]{3,2,1,0:T(8,128)} %bitcast.6, f32[128,2048]{1,0:T(8,128)} %bitcast.4, f32[1024,128]{1,0:T(8,128)} %bitcast.5, s32[1,1024]{1,0:T(1,128)} %rmap.1, f32[8,256]{1,0:T(8,128)} %rhs_r.1, f32[512,256]{1,0:T(8,128)} %rinv.1), custom_call_target="tpu_custom_call" | custom-call | tf_op jit(solution)/shard_map/pallas_call | solution.py:364
  95.8 0.0 copy-start
  95.8 1.5 %copy.10 = f32[1,128,128]{2,1,0:T(8,128)} copy(f32[1,128,128]{2,1,0:T(8,128)} %bitcast.7) | data formatting | bytes 131072
  97.3 0.0 copy-done
  97.3 0.6 copy.11
Async XLA Ops:
  95.8 1.5 %copy-start = (f32[8,256]{1,0:T(8,128)S(1)}, f32[8,256]{1,0:T(8,128)}, u32[]{:S(2)}) copy-start(f32[8,256]{1,0:T(8,128)} %get-tuple-element.9) | copy-start | bytes 24580
